TPU v7x, 256 devices: a whole 4x4x8 slice. The times are simulated.
256 devices in a mesh: dp: 32 (over z_lo, y, core), section: 8 (over z_hi, x).
Axes of the slice: x: 4, y: 4, z: 8 (z_hi: 2, z_lo: 4; z = z_hi * 4 + z_lo), core: 2. Of those that a mesh axis runs over, the one named last changes fastest.
Arguments:
- first_input: bfloat16 [8192, 2048], P('dp'), may hold values from -6 to 6
- upstream: bfloat16 [8192, 2048], P('dp'), may hold values from -6 to 6
- history: bfloat16 [8, 2, 128, 64, 2048], P('section', None, 'dp'), as said below
- example_ids: int32 [32, 4], P('dp'), may hold values from 0 to 3, each once within a row
- norm_gain: float32 [8, 2048], P('section'), may hold values from 0.1 to 1.9
- weight: bfloat16 [8, 2048, 2048], P('section', 'dp'), may hold values from -0.125 to 0.125
Outputs:
- section_outputs: bfloat16 [8, 8192, 2048], P('section', 'dp')
- block_scales: bfloat16 [8, 8192, 16], P('section', 'dp')
- weight_grad: float32 [8, 2048, 2048], P('section', 'dp')
- gain_grad: float32 [8, 2048], P('section')
Inputs may be any that keep to these rules, and one draw needn't show every extreme that they name: `example_ids`: each row names each stored example of its replica once. history[s, 1] equals history[s - 1, 0], indices of the first dimension taken modulo 8.
All inputs are finite; a program needn't handle non-finite values. Where the computation divides by a largest or mean magnitude, that divisor is 1e-20 or more.
Results may differ from a plain program's by a relative error of at most 0.038.
Values may be sent and summed in bfloat16 or wider, within the bound.
A program may use at most 64 MiB of HBM per device.

v0:
```python
import functools

import jax
import jax.numpy as jnp
from jax import lax
from jax.experimental import pallas as pl
from jax.experimental.pallas import tpu as pltpu
from jax.sharding import PartitionSpec as P

MESH = pl.DeviceIdType.MESH
D = 2048
TOK = 256
SEQ = 64
BLOCK = 128
N_SECTION = 8
NZ = 4
NY = 4
SHARD = 64
ROWS_A = 48
ROWS_B = SHARD - ROWS_A
MICRO = 16
MR = TOK // MICRO
WIDE = 32
HALF = D // 2
LAST = N_SECTION - 1
NEAR, OVER = 3, 4
LEAD_0 = 14
LEAD_7 = 16
BACK_0 = 16
BACK_7 = 0
COLS = 512
SENT = 1024
bf16 = jnp.bfloat16
f32 = jnp.float32


def relay_kernel(
    first_hbm, up_hbm, hist_hbm, ids, gain, w_hbm,
    out, scales, weight_grad, gain_out,
    shards, weight_t, hist, x_in, g_in, x_out, g_out, f_relay, b_relay, factor, normed, inv_buf, du_buf, scale_buf, gain_acc, gain_buf,
    pack, pack_out, dmixed, part_a, part_b, y_far_in, y_in, z_in, zb_in, yb_far_in, yb_in,
    local_sem, f_send, f_recv, b_send, b_recv, rf_send, rf_recv, rb_send, rb_recv,
    za_recv, ya_recv, yb_recv, zb_recv, pair_recv, ag_send,
    pack_sems, dz_send, dz_recv, gain_send, gain_recv,
    rs_send, far_recv, ring_recv, line_recv, lineb_recv, farb_recv, ringb_recv,
):
    dp = lax.axis_index("dp")
    s = lax.axis_index("section")
    zl = dp // 8
    y = lax.rem(dp // 2, NY)
    c = lax.rem(dp, 2)

    def device(zl_, y_, c_):
        return (zl_ * 8 + y_ * 2 + c_, s)

    def at_section(s_):
        return (dp, s_)

    y_up, y_dn, y_far = lax.rem(y + 1, NY), lax.rem(y + 3, NY), lax.rem(y + 2, NY)
    partner = device(zl, y, 1 - c)
    prev_dev, next_dev = at_section(lax.rem(s + 7, 8)), at_section(lax.rem(s + 1, 8))
    is_first, is_last = s == 0, s == LAST
    has_prev, has_next = s > 0, s < LAST
    direct_prev = jnp.logical_and(has_prev, s != OVER)
    direct_next = jnp.logical_and(has_next, s != NEAR)

    def z_dev(step):
        return device(lax.rem(zl + step + NZ, NZ), y, c)

    weight = shards.reshape(D, D)

    own_rows = shards.at[zl, y, c]
    load_w = pltpu.make_async_copy(w_hbm.at[0], own_rows, local_sem.at[0])
    load_w.start()
    load_hist = pltpu.make_async_copy(hist_hbm.at[0, 0], hist, local_sem.at[1])
    load_hist.start()
    load_first = pltpu.make_async_copy(first_hbm, x_in, local_sem.at[2])
    load_up = pltpu.make_async_copy(up_hbm, g_in, local_sem.at[3])
    pl.when(is_first)(load_first.start)
    pl.when(is_last)(load_up.start)

    barrier = pltpu.get_barrier_semaphore()
    z_skip = device(lax.rem(zl + 2, NZ), y, c)
    for dev in (partner, device(zl, y_up, c), device(zl, y_dn, c), device(zl, y_far, c), z_skip):
        pl.semaphore_signal(barrier, inc=1, device_id=dev, device_id_type=MESH)
    ends = jnp.logical_or(is_first, is_last)
    middle = jnp.logical_or(s == NEAR, s == OVER)
    others = (
        (z_dev(-1), zl > 0), (z_dev(1), zl < NZ - 1), (prev_dev, direct_prev), (next_dev, direct_next),
        (at_section(NEAR), ends), (at_section(OVER), ends), (at_section(0), middle), (at_section(LAST), middle),
    )
    greeted = jnp.int32(5)
    for dev, there in others:
        greeted = greeted + there.astype(jnp.int32)

        @pl.when(there)
        def _():
            pl.semaphore_signal(barrier, inc=1, device_id=dev, device_id_type=MESH)

    pl.semaphore_wait(barrier, greeted)
    load_w.wait()

    sends = []

    def piece_a(zl_, y_):
        return shards.at[zl_, y_, c, pl.ds(0, ROWS_A)]

    def piece_b(zl_, y_):
        return shards.at[zl_, y_, c, pl.ds(ROWS_A, ROWS_B)]

    def send(ref, recv_sem, dev, cond):
        copy = pltpu.make_async_remote_copy(
            src_ref=ref, dst_ref=ref, send_sem=ag_send.at[len(sends)], recv_sem=recv_sem,
            device_id=dev, device_id_type=MESH,
        )
        sends.append((copy, cond))
        if cond is None:
            copy.start()
        else:
            pl.when(cond)(copy.start)

    def arrived(ref, recv_sem, cond):
        copy = pltpu.make_async_remote_copy(
            src_ref=ref, dst_ref=ref, send_sem=ag_send.at[0], recv_sem=recv_sem,
            device_id=partner, device_id_type=MESH,
        )
        if cond is None:
            copy.wait_recv()
        else:
            pl.when(cond)(copy.wait_recv)

    def both(a, b):
        return b if a is None else jnp.logical_and(a, b)

    def in_line(z_):
        return jnp.logical_and(z_ >= 0, z_ < NZ)

    def origins(distance):
        if distance == 0:
            return [(0, zl, None)]
        if not 0 < distance < NZ:
            return []
        return [(sign, lax.rem(zl + sign * distance + 2 * NZ, NZ), in_line(zl + sign * distance)) for sign in (-1, 1)]

    def even(v):
        return lax.rem(v, 2) == 0

    def odd(v):
        return lax.rem(v, 2) == 1

    def spread_b(y_):
        for sign in (1, -1):
            send(piece_b(zl, y_), zb_recv.at[zl * NY + y_], z_dev(sign), in_line(zl + sign))

    ring_sides = ((y_dn, y_up, even), (y_up, y_dn, odd))
    for sign in (1, -1):
        send(piece_a(zl, y), za_recv.at[zl], z_dev(sign), in_line(zl + sign))
    spread_b(y)
    for y_ in (y_up, y_dn):
        send(piece_b(zl, y), yb_recv.at[y], device(zl, y_, c), None)
    for y_ in (y_up, y_dn):
        send(piece_a(zl, y), ya_recv.at[zl * NY + y], device(zl, y_, c), None)
    send(own_rows, pair_recv, partner, None)

    def line_a(distance):
        for sign, o, there in origins(distance):
            arrived(piece_a(o, y), za_recv.at[o], there)
            send(piece_a(o, y), za_recv.at[o], z_dev(-sign), both(there, in_line(zl - sign)))
            for y_ in (y_up, y_dn):
                send(piece_a(o, y), ya_recv.at[o * NY + y], device(zl, y_, c), there)
            send(piece_a(o, y), pair_recv, partner, there)

    def ring_a(distance):
        for sign, o, there in origins(distance):
            for y_from, y_to, turn in ring_sides:
                arrived(piece_a(o, y_from), ya_recv.at[o * NY + y_from], there)
                send(piece_a(o, y_from), ya_recv.at[o * NY + y_from], device(zl, y_to, c), both(there, turn(o)))
                send(piece_a(o, y_from), pair_recv, partner, there)

    def far_a(distance):
        for sign, o, there in origins(distance):
            arrived(piece_a(o, y_far), ya_recv.at[o * NY + y_far], there)
            send(piece_a(o, y_far), pair_recv, partner, there)

    def ring_b():
        for y_from, y_to, turn in ring_sides:
            arrived(piece_b(zl, y_from), yb_recv.at[y_from], None)
            send(piece_b(zl, y_from), yb_recv.at[y_from], device(zl, y_to, c), turn(zl))
            spread_b(y_from)
            send(piece_b(zl, y_from), pair_recv, partner, None)

    def far_b():
        arrived(piece_b(zl, y_far), yb_recv.at[y_far], None)
        spread_b(y_far)
        send(piece_b(zl, y_far), pair_recv, partner, None)

    def line_b(distance):
        for sign, o, there in origins(distance):
            for y_ in (y, y_dn, y_up, y_far):
                arrived(piece_b(o, y_), zb_recv.at[o * NY + y_], there)
                send(piece_b(o, y_), zb_recv.at[o * NY + y_], z_dev(-sign), both(there, in_line(zl - sign)))
                send(piece_b(o, y_), pair_recv, partner, there)

    line_a(1)
    ring_b()
    line_a(2)
    far_b()
    ring_a(0)
    ring_a(1)
    line_a(3)
    line_b(1)
    ring_a(2)
    ring_a(3)
    line_b(2)
    far_a(2)
    line_b(3)
    far_a(1)
    far_a(0)
    far_a(3)
    arrived(shards.at[pl.ds(0, NZ), pl.ds(0, NY), 1 - c], pair_recv, None)

    load_hist.wait()
    pl.when(is_first)(load_first.wait)
    pl.when(is_last)(load_up.wait)
    gain_acc[...] = jnp.zeros_like(gain_acc)

    def remote(src_ref, dst_ref, send_sem, recv_sem, dev):
        return pltpu.make_async_remote_copy(
            src_ref=src_ref, dst_ref=dst_ref, send_sem=send_sem, recv_sem=recv_sem,
            device_id=dev, device_id_type=MESH,
        )

    def rms(x):
        return lax.rsqrt(jnp.mean(x * x, axis=-1, keepdims=True) + 1e-05)

    def coded(v):
        scale = (jnp.max(jnp.abs(v), axis=-1, keepdims=True) + 1e-06).astype(bf16).astype(f32)
        return (v * (1.0 / scale)).astype(bf16).astype(f32) * scale, scale

    def rows_at(m):
        return pl.ds(pl.multiple_of(m * MR, MR), MR)

    every, low, high = pl.ds(0, D), pl.ds(0, HALF), pl.ds(HALF, HALF)

    def forward_rows(m, size, route):
        rows = pl.ds(pl.multiple_of(m * MR, MR), size)

        @pl.when(has_prev)
        def _():
            for k in range(size // MR):
                part = rows_at(m + k)
                remote(x_out.at[part], x_in.at[part], f_send.at[m + k], f_recv.at[m + k], prev_dev).wait_recv()

        x = x_in[rows, :].astype(f32)
        inverse = rms(x)
        inv_buf[rows, :] = jnp.broadcast_to(inverse, (size, BLOCK))
        nrm = (x * inverse * gain[...]).astype(bf16)
        normed[rows, :] = nrm
        slot = ids[0, m * MR // SEQ]
        old_rows = pl.ds(pl.multiple_of(lax.rem(m * MR, SEQ), MR), size)
        lane = lax.broadcasted_iota(jnp.int32, (size, BLOCK), 1)
        scale_rows = jnp.zeros((size, BLOCK), f32)

        def mixed(n):
            return jnp.dot(nrm, weight[:, n * COLS : (n + 1) * COLS], preferred_element_type=f32)

        ahead = mixed(0)
        for n in range(D // COLS):
            cols = slice(n * COLS, (n + 1) * COLS)
            z = ahead
            if n + 1 < D // COLS:
                ahead = mixed(n + 1)
            sig = 0.5 + 0.5 * jnp.tanh(0.5 * z)
            factor[rows, cols] = sig * (1.0 + z * (1.0 - sig))
            res = (x_in[rows, cols].astype(f32) + z * sig).astype(bf16)
            out[rows, cols] = res
            old = hist[slot, old_rows, cols].astype(f32)
            delta = res.astype(f32) - old
            for b in range(COLS // BLOCK):
                part = slice(b * BLOCK, (b + 1) * BLOCK)
                decoded, scale = coded(delta[:, part])
                scale_rows = jnp.where(lane == n * (COLS // BLOCK) + b, scale, scale_rows)
                if route is not None:
                    x_out[rows, n * COLS + b * BLOCK : n * COLS + (b + 1) * BLOCK] = (old[:, part] + decoded).astype(bf16)
            if route is not None and (n + 1) * COLS % SENT == 0:
                start = (n + 1) * COLS - SENT
                here = pl.ds(start, SENT)
                if route == "direct":
                    remote(x_out.at[rows, here], x_in.at[rows, here], f_send.at[m], f_recv.at[m], next_dev).start()
                else:
                    via = at_section(0 if start < HALF else LAST)
                    there = pl.ds(start % HALF, SENT)
                    remote(x_out.at[rows, here], f_relay.at[rows, there], f_send.at[m], rf_recv.at[m], via).start()
        scale_buf[rows, :] = scale_rows

    def backward_rows(m, size, route):
        rows = pl.ds(pl.multiple_of(m * MR, MR), size)

        @pl.when(has_next)
        def _():
            for k in range(size // MR):
                part = rows_at(m + k)
                remote(g_out.at[part], g_in.at[part], b_send.at[m + k], b_recv.at[m + k], next_dev).wait_recv()

        g = g_in[rows, :].astype(f32)
        dz = (g * factor[rows, :]).astype(bf16)
        dmixed[rows, :] = dz
        for k in range(size // MR):
            dz_copy(m + k).start()
        inverse = inv_buf[rows, 0:1]
        shared = jnp.zeros((size, BLOCK), f32)
        for n in range(D // COLS):
            cols = slice(n * COLS, (n + 1) * COLS)
            dn = jnp.dot(dz, weight_t[:, cols], preferred_element_type=f32)
            unit = x_in[rows, cols].astype(f32) * inverse
            du = dn * gain[:, cols]
            du_buf[0:size, cols] = du
            prod = du * unit
            for b in range(COLS // BLOCK):
                shared = shared + prod[:, b * BLOCK : (b + 1) * BLOCK]
            prod = dn * unit
            total = prod[0:8]
            for k in range(1, size // 8):
                total = total + prod[8 * k : 8 * k + 8]
            gain_acc[:, cols] += total

        if route is None:
            return
        mean = jnp.sum(shared, axis=-1, keepdims=True) * (1.0 / D)
        for n in range(D // SENT):
            for b in range(SENT // BLOCK):
                part = slice(n * SENT + b * BLOCK, n * SENT + (b + 1) * BLOCK)
                unit = x_in[rows, part].astype(f32) * inverse
                dx = g_in[rows, part].astype(f32) + inverse * (du_buf[0:size, part] - unit * mean)
                decoded, _ = coded(dx)
                g_out[rows, part] = decoded.astype(bf16)
            here = pl.ds(n * SENT, SENT)
            for k in range(size // MR):
                sub = rows_at(m + k)
                if route == "direct":
                    remote(g_out.at[sub, here], g_in.at[sub, here], b_send.at[m + k], b_recv.at[m + k], prev_dev).start()
                else:
                    via = at_section(0 if n * SENT < HALF else LAST)
                    there = pl.ds(n * SENT % HALF, SENT)
                    remote(g_out.at[sub, here], b_relay.at[sub, there], b_send.at[m + k], rb_recv.at[m + k], via).start()

    def dz_copy(m):
        here = rows_at(m)
        there = pl.ds(pl.multiple_of(TOK + m * MR, MR), MR)
        return remote(dmixed.at[here], dmixed.at[there], dz_send.at[m], dz_recv.at[m], partner)

    def relay_forward(m, _):
        rows = rows_at(m)

        def passed(cols):
            return remote(f_relay.at[rows], x_in.at[rows, cols], rf_send.at[m], f_recv.at[m], at_section(OVER))

        remote(f_relay.at[rows], f_relay.at[rows], rf_send.at[m], rf_recv.at[m], at_section(NEAR)).wait_recv()
        pl.when(is_first)(passed(low).start)
        pl.when(is_last)(passed(high).start)
        return 0

    def relay_backward(m, _):
        rows = rows_at(m)

        def passed(cols):
            return remote(b_relay.at[rows], g_in.at[rows, cols], rb_send.at[m], b_recv.at[m], at_section(NEAR))

        remote(b_relay.at[rows], b_relay.at[rows], rb_send.at[m], rb_recv.at[m], at_section(OVER)).wait_recv()
        pl.when(is_first)(passed(low).start)
        pl.when(is_last)(passed(high).start)
        return 0

    def transpose_weight(i, _):
        rows = pl.ds(pl.multiple_of(i * 256, 256), 256)
        for j in range(D // 256):
            weight_t[j * 256 : (j + 1) * 256, rows] = weight[rows, j * 256 : (j + 1) * 256].T
        return 0

    def pack_normed(m, _):
        rows = rows_at(m)
        lane = lax.broadcasted_iota(jnp.int32, (MR, BLOCK), 1)
        for t in range(D // 256):
            a = normed[rows, 256 * t : 256 * t + 128].astype(f32)
            b = normed[rows, 256 * t + 128 : 256 * t + 256].astype(f32)
            zero = jnp.where(lane < SHARD, a, pltpu.roll(b, SHARD, 1))
            one = jnp.where(lane < SHARD, pltpu.roll(a, SHARD, 1), b)
            pack[rows, 128 * t : 128 * t + 128] = jnp.where(c == 0, zero, one).astype(bf16)
            pack_out[rows, 128 * t : 128 * t + 128] = jnp.where(c == 0, one, zero).astype(bf16)
        return 0

    pack_copy = remote(pack_out, pack.at[pl.ds(TOK, TOK)], pack_sems.at[0], pack_sems.at[1], partner)

    def forward_all(route):
        def step(m, _):
            forward_rows(m, MR, route)
            if route == "direct":
                @pl.when(jnp.logical_and(is_first, m >= LEAD_0))
                def _():
                    relay_forward(m - LEAD_0, 0)
            return 0

        lax.fori_loop(0, MICRO, step, 0)

    def backward_all(route):
        def step(m, _):
            backward_rows(m, MR, route)
            if route is None:
                @pl.when(m < MICRO - BACK_0)
                def _():
                    relay_backward(m + BACK_0, 0)
            return 0

        lax.fori_loop(0, MICRO, step, 0)

    def turn_step(i, _):
        forward_rows(i * (WIDE // MR), WIDE, None)

        @pl.when(i < (MICRO - LEAD_7) // 2)
        def _():
            relay_forward(LEAD_7 + 2 * i, 0)

        backward_rows(i * (WIDE // MR), WIDE, "direct")

        @pl.when(i < (MICRO - LEAD_7) // 2)
        def _():
            relay_forward(LEAD_7 + 2 * i + 1, 0)

        @pl.when(i == TOK // WIDE - 2)
        def _():
            lax.fori_loop(0, BACK_7, relay_backward, 0)

        return 0

    @pl.when(s >= OVER)
    def _():
        lax.fori_loop(0, D // 256, transpose_weight, 0)

    @pl.when(is_last)
    def _():
        lax.fori_loop(0, LEAD_7, relay_forward, 0)
        lax.fori_loop(0, TOK // WIDE, turn_step, 0)
        lax.fori_loop(BACK_7, MICRO, relay_backward, 0)

    @pl.when(direct_next)
    def _():
        forward_all("direct")

    @pl.when(s == NEAR)
    def _():
        forward_all("relay")

    @pl.when(is_first)
    def _():
        lax.fori_loop(MICRO - LEAD_0, MICRO, relay_forward, 0)

    @pl.when(s < OVER)
    def _():
        lax.fori_loop(0, D // 256, transpose_weight, 0)
        lax.fori_loop(0, MICRO, pack_normed, 0)
        pack_copy.start()
        scales[...] = scale_buf[...].T[: D // BLOCK].astype(bf16)

    @pl.when(is_first)
    def _():
        lax.fori_loop(0, BACK_0, relay_backward, 0)
        backward_all(None)

    @pl.when(jnp.logical_and(direct_prev, has_next))
    def _():
        backward_all("direct")

    @pl.when(s == OVER)
    def _():
        backward_all("relay")

    @pl.when(s >= OVER)
    def _():
        lax.fori_loop(0, MICRO, pack_normed, 0)
        pack_copy.start()
        scales[...] = scale_buf[...].T[: D // BLOCK].astype(bf16)

    pack_copy.wait_recv()
    for m in range(MICRO):
        dz_copy(m).wait_recv()
    scatter = []

    def hand(src_ref, dst_ref, recv_sem, dev, cond=None):
        copy = remote(src_ref, dst_ref, rs_send.at[len(scatter)], recv_sem, dev)
        scatter.append((copy, cond))
        if cond is None:
            copy.start()
        else:
            pl.when(cond)(copy.start)

    def landed(ref, recv_sem, cond=None):
        copy = remote(ref, ref, rs_send.at[0], recv_sem, partner)
        if cond is None:
            copy.wait_recv()
        else:
            pl.when(cond)(copy.wait_recv)

    def add_to(ref, *terms):
        total = ref[...].astype(f32)
        for term in terms:
            total = total + term[...].astype(f32)
        ref[...] = total.astype(ref.dtype)

    low_half = zl < 2
    order = (
        jnp.where(low_half, 3, 0), jnp.where(low_half, 2, 1), jnp.where(low_half, 1 - zl, 5 - zl), zl,
    )
    up_dev, dn_dev = device(zl, y_up, c), device(zl, y_dn, c)

    def line(k):
        right = order[k] > zl
        upstream = jnp.where(right, zl > 0, zl < NZ - 1)
        return right, upstream, jnp.where(right, 0, 1)

    def b_rows(y_):
        return pl.ds(pl.multiple_of(y_ * ROWS_B, ROWS_B), ROWS_B)

    def send_line_b(k, cond):
        right, _, side = line(k)
        zd = order[k]
        for step, way in ((1, right), (-1, jnp.logical_not(right))):
            hand(part_b.at[zd], zb_in.at[side, zd], lineb_recv.at[side * NZ + zd], z_dev(step), both(cond, way))

    def send_line_a(k, cond):
        right, _, side = line(k)
        zd = order[k]
        for step, way in ((1, right), (-1, jnp.logical_not(right))):
            hand(part_a.at[zd, y], z_in.at[side, zd], line_recv.at[side * NZ + zd], z_dev(step), both(cond, way))

    def pass_line_b(k):
        _, upstream, side = line(k)
        zd = order[k]
        landed(zb_in.at[side, zd], lineb_recv.at[side * NZ + zd], upstream)

        @pl.when(upstream)
        def _():
            add_to(part_b.at[zd], zb_in.at[side, zd])

        send_line_b(k, upstream)

    def own_line_b():
        for side, there in ((0, zl > 0), (1, zl < NZ - 1)):
            landed(zb_in.at[side, zl], lineb_recv.at[side * NZ + zl], there)

            @pl.when(there)
            def _():
                add_to(part_b.at[zl], zb_in.at[side, zl])

        for dev, way in ((up_dev, even(zl)), (dn_dev, odd(zl))):
            hand(part_b.at[zl, b_rows(y_far)], yb_far_in, farb_recv, dev, way)

    def own_line_a():
        for side, there in ((0, zl > 0), (1, zl < NZ - 1)):
            landed(z_in.at[side, zl], line_recv.at[side * NZ + zl], there)

            @pl.when(there)
            def _():
                weight_grad[0:ROWS_A, :] += z_in[side, zl].astype(f32)

    def ring_b_out():
        landed(yb_far_in, farb_recv)
        add_to(part_b.at[zl, b_rows(jnp.where(even(zl), y_up, y_dn))], yb_far_in)
        hand(part_b.at[zl, b_rows(y_up)], yb_in.at[0], ringb_recv.at[0], up_dev)
        hand(part_b.at[zl, b_rows(y_dn)], yb_in.at[1], ringb_recv.at[1], dn_dev)

    def ring_b_in():
        for side in range(2):
            landed(yb_in.at[side], ringb_recv.at[side])
        weight_grad[ROWS_A:SHARD, :] = (
            part_b[zl, b_rows(y)].astype(f32) + yb_in[0].astype(f32) + yb_in[1].astype(f32)
        )

    def pass_line_a(k):
        _, upstream, side = line(k)
        zd = order[k]
        landed(z_in.at[side, zd], line_recv.at[side * NZ + zd], upstream)

        @pl.when(upstream)
        def _():
            add_to(part_a.at[zd, y], z_in.at[side, zd])

        send_line_a(k, upstream)

    def ring_out(k):
        zd = order[k]
        landed(y_far_in.at[zd], far_recv.at[zd])
        target = jnp.where(even(zd), y_up, y_dn)
        add_to(part_a.at[zd, target], y_far_in.at[zd])
        hand(part_a.at[zd, y_up], y_in.at[zd, 0], ring_recv.at[zd * 2], up_dev)
        hand(part_a.at[zd, y_dn], y_in.at[zd, 1], ring_recv.at[zd * 2 + 1], dn_dev)

    def ring_in(k):
        zd = order[k]
        for side in range(2):
            landed(y_in.at[zd, side], ring_recv.at[zd * 2 + side])
        if k < NZ - 1:
            add_to(part_a.at[zd, y], y_in.at[zd, 0], y_in.at[zd, 1])
            send_line_a(k, jnp.logical_not(line(k)[1]))
        else:
            weight_grad[0:ROWS_A, :] = (
                part_a[zd, y].astype(f32) + y_in[zd, 0].astype(f32) + y_in[zd, 1].astype(f32)
            )

    gain_steps = (
        partner, device(zl, jnp.where(even(y), y + 1, y - 1), c), device(zl, y_far, c),
        device(jnp.where(even(zl), zl + 1, zl - 1), y, c), z_skip,
    )
    gain_buf[0] = jnp.sum(gain_acc[...], axis=0, keepdims=True)

    def gain_copy(k):
        return remote(gain_buf.at[k], gain_buf.at[6 + k], gain_send.at[k], gain_recv.at[k], gain_steps[k])

    def gain_add(k):
        gain_copy(k).wait_recv()
        gain_buf[k + 1] = gain_buf[k] + gain_buf[6 + k]
        if k + 1 < len(gain_steps):
            gain_copy(k + 1).start()

    def produce(k):
        zd = order[k]
        cols = pl.ds(pl.multiple_of(zd * 256, 256), 256)
        total = lax.dot_general(pack[:, cols], dmixed[...], (((0,), (0,)), ((), ())), preferred_element_type=f32).astype(bf16)
        for j in range(NY):
            part_a[zd, j] = total[j * SHARD : j * SHARD + ROWS_A]
            part_b[zd, j * ROWS_B : (j + 1) * ROWS_B] = total[j * SHARD + ROWS_A : (j + 1) * SHARD]
        for dev, way in ((up_dev, even(zd)), (dn_dev, odd(zd))):
            hand(part_a.at[zd, y_far], y_far_in.at[zd], far_recv.at[zd], dev, way)
        if k < NZ - 1:
            send_line_b(k, jnp.logical_not(line(k)[1]))

    produce(0)
    gain_copy(0).start()
    produce(1)
    ring_out(0)
    produce(2)
    pass_line_b(0)
    gain_add(0)
    produce(3)
    ring_out(1)
    pass_line_b(1)
    ring_in(0)
    gain_add(1)
    ring_out(2)
    pass_line_b(2)
    ring_in(1)
    gain_add(2)
    pass_line_a(0)
    own_line_b()
    gain_add(3)
    ring_out(3)
    ring_in(2)
    gain_add(4)
    ring_b_out()
    pass_line_a(1)
    pass_line_a(2)
    ring_in(3)
    ring_b_in()
    own_line_a()

    gain_out[...] = gain_buf[5]

    def drain(m, _):
        rows = rows_at(m)
        dz_copy(m).wait_send()

        @pl.when(has_next)
        def _():
            remote(x_out.at[rows], x_in.at[rows], f_send.at[m], f_recv.at[m], next_dev).wait_send()

        @pl.when(has_prev)
        def _():
            remote(g_out.at[rows], g_in.at[rows], b_send.at[m], b_recv.at[m], prev_dev).wait_send()

        @pl.when(ends)
        def _():
            remote(f_relay.at[rows], f_relay.at[rows], rf_send.at[m], rf_recv.at[m], at_section(OVER)).wait_send()
            remote(b_relay.at[rows], b_relay.at[rows], rb_send.at[m], rb_recv.at[m], at_section(NEAR)).wait_send()

        return 0

    lax.fori_loop(0, MICRO, drain, 0)
    pack_copy.wait_send()
    for k in range(len(gain_steps)):
        gain_copy(k).wait_send()
    for copy, cond in sends + scatter:
        if cond is None:
            copy.wait_send()
        else:
            pl.when(cond)(copy.wait_send)


def hand_over(*refs):
    n = len(refs) // 2
    copies = []
    for src, dst in zip(refs[:n], refs[n : 2 * n]):
        rows = src.shape[0]
        pieces = 8 if rows * src.shape[1] >= 2**17 else 1
        for k in range(pieces):
            part = pl.ds(k * (rows // pieces), rows // pieces)
            copies.append(pltpu.make_async_copy(src.at[part], dst.at[part], refs[-1].at[len(copies)]))
    for copy in copies:
        copy.start()
    for copy in copies:
        copy.wait()


def body(first_input, upstream, history, example_ids, norm_gain, weight):
    vmem = pl.BlockSpec(memory_space=pltpu.VMEM)
    anywhere = pl.BlockSpec(memory_space=pl.ANY)
    smem = pl.BlockSpec(memory_space=pltpu.SMEM)
    dma = pltpu.SemaphoreType.DMA
    out, scales, weight_grad, gain_grad = pl.pallas_call(
        relay_kernel,
        out_shape=(
            jax.ShapeDtypeStruct((TOK, D), bf16),
            jax.ShapeDtypeStruct((D // BLOCK, TOK), bf16),
            jax.ShapeDtypeStruct((SHARD, D), f32),
            jax.ShapeDtypeStruct((1, D), f32),
        ),
        in_specs=[anywhere, anywhere, anywhere, smem, vmem, anywhere],
        out_specs=(vmem,) * 4,
        scratch_shapes=[
            pltpu.VMEM((NZ, NY, 2, SHARD, D), bf16),
            pltpu.VMEM((D, D), bf16),
            pltpu.VMEM((4, SEQ, D), bf16),
            pltpu.VMEM((TOK, D), bf16),
            pltpu.VMEM((TOK, D), bf16),
            pltpu.VMEM((TOK, D), bf16),
            pltpu.VMEM((TOK, D), bf16),
            pltpu.VMEM((TOK, HALF), bf16),
            pltpu.VMEM((TOK, HALF), bf16),
            pltpu.VMEM((TOK, D), f32),
            pltpu.VMEM((TOK, D), bf16),
            pltpu.VMEM((TOK, BLOCK), f32),
            pltpu.VMEM((WIDE, D), f32),
            pltpu.VMEM((TOK, BLOCK), f32),
            pltpu.VMEM((8, D), f32),
            pltpu.VMEM((11, 1, D), f32),
            pltpu.VMEM((2 * TOK, HALF), bf16),
            pltpu.VMEM((TOK, HALF), bf16),
            pltpu.VMEM((2 * TOK, D), bf16),
            pltpu.VMEM((NZ, NY, ROWS_A, D), bf16),
            pltpu.VMEM((NZ, NY * ROWS_B, D), bf16),
            pltpu.VMEM((NZ, ROWS_A, D), bf16),
            pltpu.VMEM((NZ, 2, ROWS_A, D), bf16),
            pltpu.VMEM((2, NZ, ROWS_A, D), bf16),
            pltpu.VMEM((2, NZ, NY * ROWS_B, D), bf16),
            pltpu.VMEM((ROWS_B, D), bf16),
            pltpu.VMEM((2, ROWS_B, D), bf16),
            dma((4,)),
            dma((MICRO,)), dma((MICRO,)), dma((MICRO,)), dma((MICRO,)),
            dma((MICRO,)), dma((MICRO,)), dma((MICRO,)), dma((MICRO,)),
            dma((NZ,)), dma((NZ * NY,)), dma((NY,)), dma((NZ * NY,)), dma(()), dma((136,)),
            dma((2,)), dma((MICRO,)), dma((MICRO,)), dma((5,)), dma((5,)),
            dma((96,)), dma((NZ,)), dma((NZ * 2,)), dma((2 * NZ,)), dma((2 * NZ,)), dma(()), dma((2,)),
        ],
        compiler_params=pltpu.CompilerParams(
            collective_id=0, has_side_effects=True, vmem_limit_bytes=56 * 2**20
        ),
    )(first_input, upstream, history, example_ids, norm_gain, weight)
    results = (out, scales, weight_grad, gain_grad)
    out, scales, weight_grad, gain_grad = pl.pallas_call(
        hand_over,
        out_shape=tuple(jax.ShapeDtypeStruct(r.shape, r.dtype) for r in results),
        in_specs=[vmem] * 4,
        out_specs=(anywhere,) * 4,
        scratch_shapes=[dma((18,))],
    )(*results)
    return (out[None], scales.T[None], weight_grad[None], gain_grad)


def solution(mesh):
    return jax.shard_map(
        body,
        mesh=mesh,
        in_specs=(
            P("dp", None),
            P("dp", None),
            P("section", None, "dp", None, None),
            P("dp", None),
            P("section", None),
            P("section", "dp", None),
        ),
        out_specs=(
            P("section", "dp", None),
            P("section", "dp", None),
            P("section", "dp", None),
            P("section", None),
        ),
        check_vma=False,
    )
```

profile of v0, /device:TPU:32, one launch (start us, length us, event | category | flops | bytes accessed | tf_op | source)
XLA Modules:
  0.0 204.1 jit_solution(12215824145771844314)
XLA Ops:
  0.6 200.6 %shard_map.93 = (bf16[256,2048]{1,0:T(8,128)(2,1)}, bf16[16,256]{1,0:T(8,128)(2,1)}, f32[64,2048]{1,0:T(8,128)}, f32[1,2048]{1,0:T(1,128)}) custom-call(bf16[256,2048]{1,0:T(8,128)(2,1)} %first_hbm.1, bf16[256,2048]{1,0:T(8,128)(2,1)} %up_hbm.1, bf16[1,2,4,64,2048]{4,3,2,1,0:T(8,128)(2,1)} %hist_hbm.1, s32[1,4]{1,0:T(1,128)} %ids.1, f32[1,2048]{1,0:T(1,128)} %gain.1, ...), custom_call_target="tpu_custom_call" | custom-call | tf_op jit(solution)/shard_map/pallas_call | solution.py:717
  201.3 2.7 %shard_map.94 = (bf16[256,2048]{1,0:T(8,128)(2,1)}, bf16[16,256]{1,0:T(8,128)(2,1)}, f32[64,2048]{1,0:T(8,128)}, f32[1,2048]{1,0:T(1,128)}) custom-call(bf16[256,2048]{1,0:T(8,128)(2,1)} %get-tuple-element.12.refs_0_, bf16[16,256]{1,0:T(8,128)(2,1)} %get-tuple-element.13.refs_1_, f32[64,2048]{1,0:T(8,128)} %get-tuple-element.14.refs_2_, ...), custom_call_target="tpu_custom_call" | custom-call | tf_op jit(solution)/shard_map/pallas_call | solution.py:767
where the time goes:
time: 204 us
  Pallas kernels  203 us (100%)
    pallas_call x1, Pallas kernels, body(): pl.pallas_call(relay_kernel, out_shape=(jax.ShapeDtypeStruct((TOK, D), bf...  201 us

commit v1 on v0

--- a/solution.py
+++ b/solution.py
@@ -24,7 +24,7 @@
 HALF = D // 2
 LAST = N_SECTION - 1
 NEAR, OVER = 3, 4
-LEAD_0 = 14
+LEAD_0 = 13
 LEAD_7 = 16
 BACK_0 = 16
 BACK_7 = 0
@@ -432,9 +432,44 @@
 
         return 0
 
+    def drain_gather():
+        for copy, cond in sends:
+            if cond is None:
+                copy.wait_send()
+            else:
+                pl.when(cond)(copy.wait_send)
+
+    def drain_forward(m, _):
+        rows = rows_at(m)
+
+        @pl.when(has_next)
+        def _():
+            remote(x_out.at[rows], x_in.at[rows], f_send.at[m], f_recv.at[m], next_dev).wait_send()
+
+        @pl.when(ends)
+        def _():
+            remote(f_relay.at[rows], f_relay.at[rows], rf_send.at[m], rf_recv.at[m], at_section(OVER)).wait_send()
+
+        return 0
+
+    def drain_backward(m, _):
+        rows = rows_at(m)
+        dz_copy(m).wait_send()
+
+        @pl.when(has_prev)
+        def _():
+            remote(g_out.at[rows], g_in.at[rows], b_send.at[m], b_recv.at[m], prev_dev).wait_send()
+
+        @pl.when(ends)
+        def _():
+            remote(b_relay.at[rows], b_relay.at[rows], rb_send.at[m], rb_recv.at[m], at_section(NEAR)).wait_send()
+
+        return 0
+
     @pl.when(s >= OVER)
     def _():
         lax.fori_loop(0, D // 256, transpose_weight, 0)
+        drain_gather()
 
     @pl.when(is_last)
     def _():
@@ -459,6 +494,8 @@
         lax.fori_loop(0, D // 256, transpose_weight, 0)
         lax.fori_loop(0, MICRO, pack_normed, 0)
         pack_copy.start()
+        drain_gather()
+        lax.fori_loop(0, MICRO, drain_forward, 0)
         scales[...] = scale_buf[...].T[: D // BLOCK].astype(bf16)
 
     @pl.when(is_first)
@@ -657,41 +694,33 @@
     gain_add(4)
     ring_b_out()
     pass_line_a(1)
+    before = len(scatter)
     pass_line_a(2)
+    last_hops = len(scatter) - before
+
+    def drain_sums(start, stop):
+        for copy, cond in scatter[start:stop]:
+            if cond is None:
+                copy.wait_send()
+            else:
+                pl.when(cond)(copy.wait_send)
+
     ring_in(3)
     ring_b_in()
-    own_line_a()
-
-    gain_out[...] = gain_buf[5]
-
-    def drain(m, _):
-        rows = rows_at(m)
-        dz_copy(m).wait_send()
-
-        @pl.when(has_next)
-        def _():
-            remote(x_out.at[rows], x_in.at[rows], f_send.at[m], f_recv.at[m], next_dev).wait_send()
-
-        @pl.when(has_prev)
-        def _():
-            remote(g_out.at[rows], g_in.at[rows], b_send.at[m], b_recv.at[m], prev_dev).wait_send()
-
-        @pl.when(ends)
-        def _():
-            remote(f_relay.at[rows], f_relay.at[rows], rf_send.at[m], rf_recv.at[m], at_section(OVER)).wait_send()
-            remote(b_relay.at[rows], b_relay.at[rows], rb_send.at[m], rb_recv.at[m], at_section(NEAR)).wait_send()
-
-        return 0
-
-    lax.fori_loop(0, MICRO, drain, 0)
+    lax.fori_loop(0, MICRO, drain_backward, 0)
     pack_copy.wait_send()
     for k in range(len(gain_steps)):
         gain_copy(k).wait_send()
-    for copy, cond in sends + scatter:
-        if cond is None:
-            copy.wait_send()
-        else:
-            pl.when(cond)(copy.wait_send)
+    drain_sums(0, before)
+    own_line_a()
+
+    gain_out[...] = gain_buf[5]
+
+    drain_sums(len(scatter) - last_hops, len(scatter))
+
+    @pl.when(s >= OVER)
+    def _():
+        lax.fori_loop(0, MICRO, drain_forward, 0)
 
 
 def hand_over(*refs):

time: 204 us -> 202 us (level)
    pallas_call x1, Pallas kernels: 201 us -> 199 us  [body(): pl.pallas_call(relay_kernel, out_shape=(jax.ShapeDtypeStruct((TOK, D), bf...]
where the time goes in v1:
time: 202 us
  Pallas kernels  201 us (100%)
    pallas_call x1, Pallas kernels, body(): pl.pallas_call(relay_kernel, out_shape=(jax.ShapeDtypeStruct((TOK, D), bf...  199 us

profile of v1, /device:TPU:32, one launch (start us, length us, event | category | flops | bytes accessed | tf_op | source)
XLA Modules:
  0.0 202.0 jit_solution(12461962060224090635)
XLA Ops:
  0.6 198.6 %shard_map.93 = (bf16[256,2048]{1,0:T(8,128)(2,1)}, bf16[16,256]{1,0:T(8,128)(2,1)}, f32[64,2048]{1,0:T(8,128)}, f32[1,2048]{1,0:T(1,128)}) custom-call(bf16[256,2048]{1,0:T(8,128)(2,1)} %first_hbm.1, bf16[256,2048]{1,0:T(8,128)(2,1)} %up_hbm.1, bf16[1,2,4,64,2048]{4,3,2,1,0:T(8,128)(2,1)} %hist_hbm.1, s32[1,4]{1,0:T(1,128)} %ids.1, f32[1,2048]{1,0:T(1,128)} %gain.1, ...), custom_call_target="tpu_custom_call" | custom-call | tf_op jit(solution)/shard_map/pallas_call | solution.py:746
  199.2 2.7 %shard_map.94 = (bf16[256,2048]{1,0:T(8,128)(2,1)}, bf16[16,256]{1,0:T(8,128)(2,1)}, f32[64,2048]{1,0:T(8,128)}, f32[1,2048]{1,0:T(1,128)}) custom-call(bf16[256,2048]{1,0:T(8,128)(2,1)} %get-tuple-element.12.refs_0_, bf16[16,256]{1,0:T(8,128)(2,1)} %get-tuple-element.13.refs_1_, f32[64,2048]{1,0:T(8,128)} %get-tuple-element.14.refs_2_, ...), custom_call_target="tpu_custom_call" | custom-call | tf_op jit(solution)/shard_map/pallas_call | solution.py:796

commit v2 on v1

--- a/solution.py
+++ b/solution.py
@@ -25,7 +25,7 @@
 LAST = N_SECTION - 1
 NEAR, OVER = 3, 4
 LEAD_0 = 13
-LEAD_7 = 16
+LEAD_7 = 14
 BACK_0 = 16
 BACK_7 = 0
 COLS = 512

time: 202 us -> 203 us (level)
  no operation moved by 1% of the time
where the time goes in v2:
time: 203 us
  Pallas kernels  202 us (100%)
    pallas_call x1, Pallas kernels, body(): pl.pallas_call(relay_kernel, out_shape=(jax.ShapeDtypeStruct((TOK, D), bf...  199 us

profile of v2, /device:TPU:32, one launch (start us, length us, event | category | flops | bytes accessed | tf_op | source)
XLA Modules:
  0.0 202.9 jit_solution(15087302314038551883)
XLA Ops:
  0.6 199.4 %shard_map.93 = (bf16[256,2048]{1,0:T(8,128)(2,1)}, bf16[16,256]{1,0:T(8,128)(2,1)}, f32[64,2048]{1,0:T(8,128)}, f32[1,2048]{1,0:T(1,128)}) custom-call(bf16[256,2048]{1,0:T(8,128)(2,1)} %first_hbm.1, bf16[256,2048]{1,0:T(8,128)(2,1)} %up_hbm.1, bf16[1,2,4,64,2048]{4,3,2,1,0:T(8,128)(2,1)} %hist_hbm.1, s32[1,4]{1,0:T(1,128)} %ids.1, f32[1,2048]{1,0:T(1,128)} %gain.1, ...), custom_call_target="tpu_custom_call" | custom-call | tf_op jit(solution)/shard_map/pallas_call | solution.py:746
  200.1 2.7 %shard_map.94 = (bf16[256,2048]{1,0:T(8,128)(2,1)}, bf16[16,256]{1,0:T(8,128)(2,1)}, f32[64,2048]{1,0:T(8,128)}, f32[1,2048]{1,0:T(1,128)}) custom-call(bf16[256,2048]{1,0:T(8,128)(2,1)} %get-tuple-element.12.refs_0_, bf16[16,256]{1,0:T(8,128)(2,1)} %get-tuple-element.13.refs_1_, f32[64,2048]{1,0:T(8,128)} %get-tuple-element.14.refs_2_, ...), custom_call_target="tpu_custom_call" | custom-call | tf_op jit(solution)/shard_map/pallas_call | solution.py:796
